TPU v7x, 512 devices: a whole 4x8x8 slice. The times are simulated.
512 devices in a mesh: section: 8 (over x, core), expert: 64 (over z, y).
Axes of the slice: x: 4, y: 8, z: 8, core: 2. Of those that a mesh axis runs over, the one named last changes fastest.
Arguments:
- micro_inputs: bfloat16 [15, 256, 3584], P(None, 'expert'), may hold values from -6 to 6
- norm_gain: bfloat16 [8, 3584], P('section'), may hold values from 0.25 to 1.75
- gate_up: bfloat16 [8, 64, 3584, 256], P('section', 'expert'), may hold values from -0.09375 to 0.09375
- down_proj: bfloat16 [8, 64, 128, 3584], P('section', 'expert'), may hold values from -0.1875 to 0.1875
- routes: int32 [8, 8, 256, 2], P('section', None, 'expert'), may hold values from 0 to 7, all different within a row; in each aligned block of 4 rows (0 to 3, 4 to 7, ..., all dimensions but the last counted through in order) at most 2 rows name the same one
- route_weights: float32 [8, 8, 256, 2], P('section', None, 'expert'), may hold values from 0.25 to 1
Outputs:
- layer_outputs: bfloat16 [8, 8, 256, 3584], P('section', None, 'expert')
Inputs may be any that keep to these rules, and one draw needn't show every extreme that they name: `routes`: in each layer and tick, among the rows of one device no expert is picked by more than 2 rows, a bound that some block reaches; each row picks 2 distinct experts.
All inputs are finite; a program needn't handle non-finite values.
Results may differ from a plain program's by a relative error of at most 0.029.
Values may be sent and summed in bfloat16 or wider, within the bound.
A program may use at most 64 MiB of HBM per device.

v0:
```python
import jax
import jax.numpy as jnp
from jax import lax
from jax.sharding import PartitionSpec as P

SHARDS = 8


EPSILON = 1e-06


def from_behind(value, axis, steps):
    count = lax.axis_size(axis)
    leading, last = (max(0, -steps), min(count, count - steps))
    return lax.ppermute(value, axis, [(source, source + steps) for source in range(leading, last)])


def rms_normed(row_block, gain_row):
    values = row_block.astype(jnp.float32)
    scaled = values * lax.rsqrt(jnp.mean(values * values, axis=1, keepdims=True) + EPSILON)
    return (scaled * gain_row.astype(jnp.float32)).astype(jnp.bfloat16)


def slot_tables(picked, experts, capacity):
    row_count, pick_count = picked.shape
    flat_picks = picked.reshape(-1)
    order_index = jnp.arange(row_count * pick_count, dtype=jnp.int32)
    earlier = (flat_picks[None, :] == flat_picks[:, None]) & (
        order_index[None, :] < order_index[:, None]
    )
    slot_index = jnp.sum(earlier.astype(jnp.int32), axis=1).reshape(row_count, pick_count)
    hit_expert = (picked[:, :, None] == jnp.arange(experts, dtype=jnp.int32)[None, None, :]).astype(
        jnp.float32
    )
    hit_slot = (
        slot_index[:, :, None] == jnp.arange(capacity, dtype=jnp.int32)[None, None, :]
    ).astype(jnp.float32)
    return (hit_expert, hit_slot)


def slice_forward(received, gate_slice, down_slice):
    feature_count = received.shape[-1]
    unit_count = down_slice.shape[0]
    stacked = received.reshape(-1, feature_count)
    projected = jnp.dot(stacked, gate_slice, preferred_element_type=jnp.float32)
    hidden_units = (jax.nn.silu(projected[:, :unit_count]) * projected[:, unit_count:]).astype(
        jnp.bfloat16
    )
    partial_out = jnp.dot(hidden_units, down_slice, preferred_element_type=jnp.float32).astype(
        jnp.bfloat16
    )
    return partial_out.reshape(received.shape[:-1] + (down_slice.shape[1],))


def return_partials(partial_rows):
    return lax.all_to_all(partial_rows, "expert", split_axis=0, concat_axis=0, tiled=True)


def expert_layer(current, gain_row, gate_slice, down_slice, picked, picked_weights):
    row_count, pick_count = picked.shape
    feature_count = current.shape[1]
    devices = lax.axis_size("expert")
    experts = devices // SHARDS
    capacity = min(row_count, max(2, 2 * ((row_count * pick_count + experts - 1) // experts)))
    normed = rms_normed(current, gain_row)
    hit_expert, hit_slot = slot_tables(picked, experts, capacity)
    placement = jnp.einsum("rke,rkc->ecr", hit_expert, hit_slot).astype(jnp.bfloat16)
    outgoing = jnp.einsum(
        "ecr,rd->ecd", placement, normed, preferred_element_type=jnp.float32
    ).astype(jnp.bfloat16)
    copies = jnp.repeat(outgoing, SHARDS, axis=0)
    returned = return_partials(
        slice_forward(
            lax.all_to_all(copies, "expert", split_axis=0, concat_axis=0, tiled=True),
            gate_slice,
            down_slice,
        )
    )
    totals = jnp.sum(
        returned.astype(jnp.float32).reshape(experts, SHARDS, capacity, feature_count), axis=1
    )
    mixing = jnp.einsum("rke,rkc,rk->rec", hit_expert, hit_slot, picked_weights)
    routed = jnp.einsum("rec,ecd->rd", mixing, totals, precision=lax.Precision.HIGHEST)
    return (current.astype(jnp.float32) + routed).astype(jnp.bfloat16)


def body(micro_inputs, norm_gain, gate_up, down_proj, routes, route_weights):
    section_index = lax.axis_index("section")
    section_count = lax.axis_size("section")
    gain_row = norm_gain[0]
    gate_slice = gate_up[0, 0]
    down_slice = down_proj[0, 0]
    first_index = jnp.where(section_index == 0, 0, section_count + section_index - 1)
    current = lax.dynamic_index_in_dim(micro_inputs, first_index, 0, keepdims=False)
    produced = []
    output_rows = current
    for tick_index in range(section_count):
        if tick_index > 0:
            arrived = from_behind(output_rows, "section", 1)
            current = jnp.where(section_index == 0, micro_inputs[tick_index], arrived)
        output_rows = expert_layer(
            current,
            gain_row,
            gate_slice,
            down_slice,
            routes[0, tick_index],
            route_weights[0, tick_index],
        )
        produced.append(output_rows)
    return jnp.stack(produced)[None]


def solution(mesh):
    return jax.shard_map(
        body,
        mesh=mesh,
        in_specs=(
            P(None, "expert", None),
            P("section", None),
            P("section", "expert", None, None),
            P("section", "expert", None, None),
            P("section", None, "expert", None),
            P("section", None, "expert", None),
        ),
        out_specs=P("section", None, "expert", None),
        check_vma=False,
    )
```

profile of v0, /device:TPU:8, one launch (start us, length us, event | category | flops | bytes accessed | tf_op | source)
XLA Modules:
  0.0 666.4 jit_solution(182360006541022145)
XLA Ops:
  5.8 42.9 %all_to_all.80 = bf16[64,2,3584]{2,1,0:T(2,128)(2,1)S(1)} all-to-all(bf16[64,2,3584]{2,1,0:T(2,128)(2,1)S(1)} %bitcast.230), channel_id=1, replica_groups=mesh['section'=8,'expert'=64] {'expert'}, dimensions={0} | all-to-all | bytes 1835008 | tf_op jit(solution)/shard_map/all_to_all | solution.py:74
  56.2 7.0 %all-to-all-start.1 = ((bf16[64,2,3584]{2,1,0:T(2,128)(2,1)}), bf16[64,2,3584]{2,1,0:T(2,128)(2,1)}, u32[]{:S(2)}, u32[]{:S(2)}) async-start(bf16[64,2,3584]{2,1,0:T(2,128)(2,1)} %reshape.220), calls=%async_computation.1 | async-start | bytes 1835008 | tf_op jit(solution)/shard_map/all_to_all | solution.py:56
  64.2 24.9 %all-to-all-done.1 = bf16[64,2,3584]{2,1,0:T(2,128)(2,1)} async-done(((bf16[64,2,3584]{2,1,0:T(2,128)(2,1)}), bf16[64,2,3584]{2,1,0:T(2,128)(2,1)}, u32[]{:S(2)}, u32[]{:S(2)}) %all-to-all-start.1) | async-done | bytes 917536 | tf_op jit(solution)/shard_map/all_to_all | solution.py:56
  94.7 33.1 %all_to_all.81 = bf16[64,2,3584]{2,1,0:T(2,128)(2,1)} all-to-all(bf16[64,2,3584]{2,1,0:T(2,128)(2,1)S(1)} %bitcast.231), channel_id=1, replica_groups=mesh['section'=8,'expert'=64] {'expert'}, dimensions={0} | all-to-all | bytes 1835008 | tf_op jit(solution)/shard_map/all_to_all | solution.py:74
  127.8 3.2 reshape.224
  137.0 7.6 %all-to-all-start.3 = ((bf16[64,2,3584]{2,1,0:T(2,128)(2,1)}), bf16[64,2,3584]{2,1,0:T(2,128)(2,1)}, u32[]{:S(2)}, u32[]{:S(2)}) async-start(bf16[64,2,3584]{2,1,0:T(2,128)(2,1)} %reshape.225), calls=%async_computation.3 | async-start | bytes 1835008 | tf_op jit(solution)/shard_map/all_to_all | solution.py:56
  145.6 26.5 %all-to-all-done.3 = bf16[64,2,3584]{2,1,0:T(2,128)(2,1)} async-done(((bf16[64,2,3584]{2,1,0:T(2,128)(2,1)}), bf16[64,2,3584]{2,1,0:T(2,128)(2,1)}, u32[]{:S(2)}, u32[]{:S(2)}) %all-to-all-start.3) | async-done | bytes 917536 | tf_op jit(solution)/shard_map/all_to_all | solution.py:56
  177.6 35.2 %all_to_all.82 = bf16[64,2,3584]{2,1,0:T(2,128)(2,1)} all-to-all(bf16[64,2,3584]{2,1,0:T(2,128)(2,1)S(1)} %bitcast.232), channel_id=1, replica_groups=mesh['section'=8,'expert'=64] {'expert'}, dimensions={0} | all-to-all | bytes 1835008 | tf_op jit(solution)/shard_map/all_to_all | solution.py:74
  212.9 3.2 reshape.229
  222.1 8.5 %all-to-all-start.5 = ((bf16[64,2,3584]{2,1,0:T(2,128)(2,1)}), bf16[64,2,3584]{2,1,0:T(2,128)(2,1)}, u32[]{:S(2)}, u32[]{:S(2)}) async-start(bf16[64,2,3584]{2,1,0:T(2,128)(2,1)} %reshape.230), calls=%async_computation.5 | async-start | bytes 1835008 | tf_op jit(solution)/shard_map/all_to_all | solution.py:56
  231.5 25.4 %all-to-all-done.5 = bf16[64,2,3584]{2,1,0:T(2,128)(2,1)} async-done(((bf16[64,2,3584]{2,1,0:T(2,128)(2,1)}), bf16[64,2,3584]{2,1,0:T(2,128)(2,1)}, u32[]{:S(2)}, u32[]{:S(2)}) %all-to-all-start.5) | async-done | bytes 917536 | tf_op jit(solution)/shard_map/all_to_all | solution.py:56
  262.5 33.6 %all_to_all.83 = bf16[64,2,3584]{2,1,0:T(2,128)(2,1)} all-to-all(bf16[64,2,3584]{2,1,0:T(2,128)(2,1)S(1)} %bitcast.233), channel_id=1, replica_groups=mesh['section'=8,'expert'=64] {'expert'}, dimensions={0} | all-to-all | bytes 1835008 | tf_op jit(solution)/shard_map/all_to_all | solution.py:74
  296.1 3.2 reshape.234
  305.3 7.1 %all-to-all-start.7 = ((bf16[64,2,3584]{2,1,0:T(2,128)(2,1)}), bf16[64,2,3584]{2,1,0:T(2,128)(2,1)}, u32[]{:S(2)}, u32[]{:S(2)}) async-start(bf16[64,2,3584]{2,1,0:T(2,128)(2,1)} %reshape.235), calls=%async_computation.7 | async-start | bytes 1835008 | tf_op jit(solution)/shard_map/all_to_all | solution.py:56
  313.4 25.0 %all-to-all-done.7 = bf16[64,2,3584]{2,1,0:T(2,128)(2,1)} async-done(((bf16[64,2,3584]{2,1,0:T(2,128)(2,1)}), bf16[64,2,3584]{2,1,0:T(2,128)(2,1)}, u32[]{:S(2)}, u32[]{:S(2)}) %all-to-all-start.7) | async-done | bytes 917536 | tf_op jit(solution)/shard_map/all_to_all | solution.py:56
  343.9 33.7 %all_to_all.84 = bf16[64,2,3584]{2,1,0:T(2,128)(2,1)} all-to-all(bf16[64,2,3584]{2,1,0:T(2,128)(2,1)S(1)} %bitcast.234), channel_id=1, replica_groups=mesh['section'=8,'expert'=64] {'expert'}, dimensions={0} | all-to-all | bytes 1835008 | tf_op jit(solution)/shard_map/all_to_all | solution.py:74
  377.6 3.2 reshape.239
  386.8 7.1 %all-to-all-start.9 = ((bf16[64,2,3584]{2,1,0:T(2,128)(2,1)}), bf16[64,2,3584]{2,1,0:T(2,128)(2,1)}, u32[]{:S(2)}, u32[]{:S(2)}) async-start(bf16[64,2,3584]{2,1,0:T(2,128)(2,1)} %reshape.240), calls=%async_computation.9 | async-start | bytes 1835008 | tf_op jit(solution)/shard_map/all_to_all | solution.py:56
  394.9 25.0 %all-to-all-done.9 = bf16[64,2,3584]{2,1,0:T(2,128)(2,1)} async-done(((bf16[64,2,3584]{2,1,0:T(2,128)(2,1)}), bf16[64,2,3584]{2,1,0:T(2,128)(2,1)}, u32[]{:S(2)}, u32[]{:S(2)}) %all-to-all-start.9) | async-done | bytes 917536 | tf_op jit(solution)/shard_map/all_to_all | solution.py:56
  425.4 33.5 %all_to_all.85 = bf16[64,2,3584]{2,1,0:T(2,128)(2,1)} all-to-all(bf16[64,2,3584]{2,1,0:T(2,128)(2,1)S(1)} %bitcast.235), channel_id=1, replica_groups=mesh['section'=8,'expert'=64] {'expert'}, dimensions={0} | all-to-all | bytes 1835008 | tf_op jit(solution)/shard_map/all_to_all | solution.py:74
  458.9 3.2 reshape.244
  468.1 7.4 %all-to-all-start.11 = ((bf16[64,2,3584]{2,1,0:T(2,128)(2,1)}), bf16[64,2,3584]{2,1,0:T(2,128)(2,1)}, u32[]{:S(2)}, u32[]{:S(2)}) async-start(bf16[64,2,3584]{2,1,0:T(2,128)(2,1)} %reshape.245), calls=%async_computation.11 | async-start | bytes 1835008 | tf_op jit(solution)/shard_map/all_to_all | solution.py:56
  476.5 24.8 %all-to-all-done.11 = bf16[64,2,3584]{2,1,0:T(2,128)(2,1)} async-done(((bf16[64,2,3584]{2,1,0:T(2,128)(2,1)}), bf16[64,2,3584]{2,1,0:T(2,128)(2,1)}, u32[]{:S(2)}, u32[]{:S(2)}) %all-to-all-start.11) | async-done | bytes 917536 | tf_op jit(solution)/shard_map/all_to_all | solution.py:56
  506.9 33.5 %all_to_all.86 = bf16[64,2,3584]{2,1,0:T(2,128)(2,1)} all-to-all(bf16[64,2,3584]{2,1,0:T(2,128)(2,1)S(1)} %bitcast.236), channel_id=1, replica_groups=mesh['section'=8,'expert'=64] {'expert'}, dimensions={0} | all-to-all | bytes 1835008 | tf_op jit(solution)/shard_map/all_to_all | solution.py:74
  540.4 3.2 reshape.249
  549.7 7.1 %all-to-all-start.13 = ((bf16[64,2,3584]{2,1,0:T(2,128)(2,1)}), bf16[64,2,3584]{2,1,0:T(2,128)(2,1)}, u32[]{:S(2)}, u32[]{:S(2)}) async-start(bf16[64,2,3584]{2,1,0:T(2,128)(2,1)} %reshape.250), calls=%async_computation.13 | async-start | bytes 1835008 | tf_op jit(solution)/shard_map/all_to_all | solution.py:56
  557.7 25.0 %all-to-all-done.13 = bf16[64,2,3584]{2,1,0:T(2,128)(2,1)} async-done(((bf16[64,2,3584]{2,1,0:T(2,128)(2,1)}), bf16[64,2,3584]{2,1,0:T(2,128)(2,1)}, u32[]{:S(2)}, u32[]{:S(2)}) %all-to-all-start.13) | async-done | bytes 917536 | tf_op jit(solution)/shard_map/all_to_all | solution.py:56
  588.2 33.8 %all_to_all.87 = bf16[64,2,3584]{2,1,0:T(2,128)(2,1)} all-to-all(bf16[64,2,3584]{2,1,0:T(2,128)(2,1)S(1)} %bitcast.237), channel_id=1, replica_groups=mesh['section'=8,'expert'=64] {'expert'}, dimensions={0} | all-to-all | bytes 1835008 | tf_op jit(solution)/shard_map/all_to_all | solution.py:74
  622.0 3.2 reshape.254
  628.1 3.1 reshape.255
  631.2 6.9 %all-to-all-start.15 = ((bf16[64,2,3584]{2,1,0:T(2,128)(2,1)}), bf16[64,2,3584]{2,1,0:T(2,128)(2,1)S(1)}, u32[]{:S(2)}, u32[]{:S(2)}) async-start(bf16[64,2,3584]{2,1,0:T(2,128)(2,1)} %reshape.255), calls=%async_computation.15 | async-start | bytes 1835008 | tf_op jit(solution)/shard_map/all_to_all | solution.py:56
  638.5 25.6 %all-to-all-done.15 = bf16[64,2,3584]{2,1,0:T(2,128)(2,1)S(1)} async-done(((bf16[64,2,3584]{2,1,0:T(2,128)(2,1)}), bf16[64,2,3584]{2,1,0:T(2,128)(2,1)S(1)}, u32[]{:S(2)}, u32[]{:S(2)}) %all-to-all-start.15) | async-done | bytes 917536 | tf_op jit(solution)/shard_map/all_to_all | solution.py:56
  (179 shorter events, 99.6 us)
Async XLA Ops:
  0.0 50.0 %copy-start = (bf16[1,1,3584,256]{3,2,1,0:T(8,128)(2,1)S(1)}, bf16[1,1,3584,256]{3,2,1,0:T(8,128)(2,1)}, u32[]{:S(2)}) copy-start(bf16[1,1,3584,256]{3,2,1,0:T(8,128)(2,1)} %param.8) | copy-start | bytes 5505028
  50.0 1.7 copy-start.1
  53.1 10.1 %copy-start.3 = (f32[1,8,4,2]{1,3,2,0:T(2,128)S(1)}, f32[1,8,4,2]{1,3,2,0:T(2,128)}, u32[]{:S(2)}) copy-start(f32[1,8,4,2]{1,3,2,0:T(2,128)} %param.11) | copy-start | bytes 772
  56.2 35.0 %copy-start.2 = (bf16[15,4,3584]{2,1,0:T(4,128)(2,1)S(1)}, bf16[15,4,3584]{2,1,0:T(4,128)(2,1)}, u32[]{:S(2)}) copy-start(bf16[15,4,3584]{2,1,0:T(4,128)(2,1)} %param.6) | copy-start | bytes 1290244
  56.2 33.0 %all-to-all-start.1 = ((bf16[64,2,3584]{2,1,0:T(2,128)(2,1)}), bf16[64,2,3584]{2,1,0:T(2,128)(2,1)}, u32[]{:S(2)}, u32[]{:S(2)}) async-start(bf16[64,2,3584]{2,1,0:T(2,128)(2,1)} %reshape.220), calls=%async_computation.1 | async-start | bytes 1835008 | tf_op jit(solution)/shard_map/all_to_all | solution.py:56
  91.5 2.1 collective-permute-start
  137.0 35.1 %all-to-all-start.3 = ((bf16[64,2,3584]{2,1,0:T(2,128)(2,1)}), bf16[64,2,3584]{2,1,0:T(2,128)(2,1)}, u32[]{:S(2)}, u32[]{:S(2)}) async-start(bf16[64,2,3584]{2,1,0:T(2,128)(2,1)} %reshape.225), calls=%async_computation.3 | async-start | bytes 1835008 | tf_op jit(solution)/shard_map/all_to_all | solution.py:56
  174.5 2.1 collective-permute-start.1
  222.1 34.8 %all-to-all-start.5 = ((bf16[64,2,3584]{2,1,0:T(2,128)(2,1)}), bf16[64,2,3584]{2,1,0:T(2,128)(2,1)}, u32[]{:S(2)}, u32[]{:S(2)}) async-start(bf16[64,2,3584]{2,1,0:T(2,128)(2,1)} %reshape.230), calls=%async_computation.5 | async-start | bytes 1835008 | tf_op jit(solution)/shard_map/all_to_all | solution.py:56
  259.3 2.1 collective-permute-start.2
  305.3 33.0 %all-to-all-start.7 = ((bf16[64,2,3584]{2,1,0:T(2,128)(2,1)}), bf16[64,2,3584]{2,1,0:T(2,128)(2,1)}, u32[]{:S(2)}, u32[]{:S(2)}) async-start(bf16[64,2,3584]{2,1,0:T(2,128)(2,1)} %reshape.235), calls=%async_computation.7 | async-start | bytes 1835008 | tf_op jit(solution)/shard_map/all_to_all | solution.py:56
  340.8 2.1 collective-permute-start.3
  386.8 33.0 %all-to-all-start.9 = ((bf16[64,2,3584]{2,1,0:T(2,128)(2,1)}), bf16[64,2,3584]{2,1,0:T(2,128)(2,1)}, u32[]{:S(2)}, u32[]{:S(2)}) async-start(bf16[64,2,3584]{2,1,0:T(2,128)(2,1)} %reshape.240), calls=%async_computation.9 | async-start | bytes 1835008 | tf_op jit(solution)/shard_map/all_to_all | solution.py:56
  422.3 2.1 collective-permute-start.4
  468.1 33.2 %all-to-all-start.11 = ((bf16[64,2,3584]{2,1,0:T(2,128)(2,1)}), bf16[64,2,3584]{2,1,0:T(2,128)(2,1)}, u32[]{:S(2)}, u32[]{:S(2)}) async-start(bf16[64,2,3584]{2,1,0:T(2,128)(2,1)} %reshape.245), calls=%async_computation.11 | async-start | bytes 1835008 | tf_op jit(solution)/shard_map/all_to_all | solution.py:56
  503.8 2.1 collective-permute-start.5
  549.7 33.0 %all-to-all-start.13 = ((bf16[64,2,3584]{2,1,0:T(2,128)(2,1)}), bf16[64,2,3584]{2,1,0:T(2,128)(2,1)}, u32[]{:S(2)}, u32[]{:S(2)}) async-start(bf16[64,2,3584]{2,1,0:T(2,128)(2,1)} %reshape.250), calls=%async_computation.13 | async-start | bytes 1835008 | tf_op jit(solution)/shard_map/all_to_all | solution.py:56
  585.1 2.1 collective-permute-start.6
  631.2 32.9 %all-to-all-start.15 = ((bf16[64,2,3584]{2,1,0:T(2,128)(2,1)}), bf16[64,2,3584]{2,1,0:T(2,128)(2,1)S(1)}, u32[]{:S(2)}, u32[]{:S(2)}) async-start(bf16[64,2,3584]{2,1,0:T(2,128)(2,1)} %reshape.255), calls=%async_computation.15 | async-start | bytes 1835008 | tf_op jit(solution)/shard_map/all_to_all | solution.py:56
  665.2 0.7 copy-start.4
where the time goes:
time: 675 us; the launch traced here: 666 us
  blocking collectives  279 us (41%)
  waiting for transfers between devices  207 us (31%)
  starting transfers between devices  67.7 us (10%)
  local copies, waits for them, and re-layouts  60 us (9%)
  matrix products  32 us (5%)
  other arithmetic  19.6 us (3%)
    all_to_all x8, blocking collectives, expert_layer(): lax.all_to_all(copies, 'expert', split_axis=0, concat_axis=0, tiled=True)  279 us
    all_to_all x8, waiting for transfers between devices, return_partials(): lax.all_to_all(partial_rows, 'expert', split_axis=0, concat_axis=0, tiled...  202 us
    all_to_all x8, starting transfers between devices, return_partials(): lax.all_to_all(partial_rows, 'expert', split_axis=0, concat_axis=0, tiled...  58.6 us
    reshape x8, local copies, waits for them, and re-layouts, slice_forward(): return partial_out.reshape(received.shape[:-1] + (down_slice.shape[1],))  24.6 us
    reshape x8, local copies, waits for them, and re-layouts, slice_forward(): stacked = received.reshape(-1, feature_count)  23.7 us
    reduce_sum x8, other arithmetic, expert_layer(): jnp.sum(returned.astype(jnp.float32).reshape(experts, SHARDS, capacity, f...  15.3 us
  transfers between devices with their start and end apart: 15, of which 15 were waited for; matrix products, arithmetic and copies ran while one was open for 1% of the time, Pallas kernels for 0%

commit v1 on v0

v1 whole, which is shorter than its diff:
```python
import numpy as np
import jax
import jax.numpy as jnp
from jax import lax
from jax.experimental import pallas as pl
from jax.experimental.pallas import tpu as pltpu
from jax.sharding import PartitionSpec as P

D = 3584
FF = 128
N = 8
ROWS = 4
CAP = 2
SLOT = N * CAP
CA = 512
CB = 384
WA = 4 * CA
EPSILON = 1e-06
MESH = pl.DeviceIdType.MESH
ORDER = (4, 3, 5, 2, 6, 1, 7)
BF = jnp.bfloat16
F32 = jnp.float32


def dot(a, b):
    return jnp.dot(a, b, preferred_element_type=F32)


def kernel(ent, gain, wg, wd, la, ra, lb, rb, wslot, perm, out,
           hop, na, nb, sa, sb, ba_send, bb_send, ba, bb,
           pa_send, pb_send, pa, pb, qa_send, qb_send, qa, qb, ssem, rsem, hs, hr):
    s = lax.axis_index("section")
    e = lax.axis_index("expert")
    z, y = e // N, e % N

    def on_z(d):
        return (s, ((z + d) % N) * N + y)

    def on_y(d):
        return (s, z * N + (y + d) % N)

    bar = pltpu.get_barrier_semaphore()
    for d in range(1, N):
        pl.semaphore_signal(bar, inc=1, device_id=on_z(d), device_id_type=MESH)
        pl.semaphore_signal(bar, inc=1, device_id=on_y(d), device_id_type=MESH)
    pl.semaphore_signal(bar, inc=1, device_id=((s + 1) % N, e), device_id_type=MESH)
    pl.semaphore_signal(bar, inc=1, device_id=((s + N - 1) % N, e), device_id_type=MESH)
    pl.semaphore_wait(bar, 2 * (N - 1) + 2)

    def to_peer(phase, d, src, dst, me, along):
        return pltpu.make_async_remote_copy(
            src_ref=src, dst_ref=dst.at[me], send_sem=ssem.at[phase, d], recv_sem=rsem.at[phase, d],
            device_id=along(d), device_id_type=MESH)

    def from_peer(phase, d, src, dst, me, along):
        return pltpu.make_async_remote_copy(
            src_ref=src, dst_ref=dst.at[(me + N - d) % N], send_sem=ssem.at[phase, d],
            recv_sem=rsem.at[phase, d], device_id=along(d), device_id_type=MESH)

    def hop_copy(t):
        return pltpu.make_async_remote_copy(
            src_ref=out.at[t], dst_ref=hop.at[t + 1], send_sem=hs.at[t], recv_sem=hr.at[t],
            device_id=((s + 1) % N, e), device_id_type=MESH)

    phases = (
        (lambda d: na, sa, z, on_z),
        (lambda d: nb, sb, y, on_y),
        (lambda d: ba_send, ba, y, on_y),
        (lambda d: bb_send.at[(z + d) % N], bb, z, on_z),
        (lambda d: pa_send.at[(y + d) % N], pa, y, on_y),
        (lambda d: pb_send.at[(z + d) % N], pb, z, on_z),
        (lambda d: qa_send.at[(z + d) % N], qa, z, on_z),
        (lambda d: qb_send.at[(y + d) % N], qb, y, on_y),
    )

    def start(phase):
        src, dst, me, along = phases[phase]
        for d in ORDER:
            to_peer(phase, d, src(d), dst, me, along).start()

    def arrive(phase):
        src, dst, me, along = phases[phase]
        for d in ORDER:
            from_peer(phase, d, src(d), dst, me, along).wait_recv()

    def sent(phase):
        src, dst, me, along = phases[phase]
        for d in ORDER:
            to_peer(phase, d, src(d), dst, me, along).wait_send()

    def tick(t, carry):
        @pl.when(jnp.logical_or(s == 0, t == 0))
        def _():
            out[t] = ent[t]

        @pl.when(jnp.logical_and(s > 0, t > 0))
        def _():
            hop_copy(t - 1).wait_recv()
            out[t] = hop[t]

        x = out[t].astype(F32)
        ss = jnp.sum(x * x, axis=1, keepdims=True)
        ss = ss + pltpu.roll(ss, 8, 0)
        ss = ss + pltpu.roll(ss, 4, 0)
        n = ((x * lax.rsqrt(ss * (1.0 / D) + EPSILON)) * gain[...]).astype(BF)
        na[...] = n[:, :CA]
        nb[...] = n[:, CA:]
        start(0)
        start(1)
        sa[z] = n[:, :CA]
        sb[y] = n[:, CA:]
        arrive(0)
        ba_send[...] = dot(la[t], sa[...].reshape(128, CA)).astype(BF)
        start(2)
        ba[y] = ba_send[...]
        arrive(1)
        bb_send[...] = dot(lb[t], sb[...].reshape(128, CB)).astype(BF).reshape(N, 64, CB)
        start(3)
        bb[z] = bb_send[z]
        arrive(3)
        proj_b = jnp.zeros((128, 2 * FF), F32)
        for q in range(4):
            proj_b += dot(bb[:, 16 * q:16 * q + 16, :].reshape(128, CB),
                          wg[WA + q * CB:WA + (q + 1) * CB, :])
        high = proj_b.astype(BF)
        low = (proj_b - high.astype(F32)).astype(BF)
        proj = dot(perm[...], high) + dot(perm[...], low)
        arrive(2)
        for q in range(4):
            proj += dot(ba[:, 16 * q:16 * q + 16, :].reshape(128, CA),
                        wg[q * CA:(q + 1) * CA, :])
        gate, up = proj[:, :FF], proj[:, FF:]
        inner = (gate / (1.0 + jnp.exp(-gate)) * up * wslot[t]).astype(BF)
        for q in range(4):
            pa_send[:, 16 * q:16 * q + 16, :] = dot(
                inner, wd[:, q * CA:(q + 1) * CA]).astype(BF).reshape(N, 16, CA)
        start(4)
        inner_b = dot(perm[...], inner).astype(BF)
        for q in range(4):
            pb_send[:, 16 * q:16 * q + 16, :] = dot(
                inner_b, wd[:, WA + q * CB:WA + (q + 1) * CB]).astype(BF).reshape(N, 16, CB)
        start(5)
        pa[y] = pa_send[y]
        pb[z] = pb_send[z]
        arrive(5)
        qb_send[...] = dot(rb[t], pb[...].reshape(512, CB)).astype(BF).reshape(N, 16, CB)
        start(7)
        qb[y] = qb_send[y]
        arrive(4)
        total = pa[0].astype(F32)
        for i in range(1, N):
            total += pa[i].astype(F32)
        qa_send[...] = dot(ra[t], total.astype(BF)).astype(BF).reshape(N, 16, CA)
        start(6)
        qa[z] = qa_send[z]
        arrive(7)
        total_b = qb[0].astype(F32)
        for i in range(1, N):
            total_b += qb[i].astype(F32)
        arrive(6)
        total_a = qa[0].astype(F32)
        for i in range(1, N):
            total_a += qa[i].astype(F32)
        out[t, :, :CA] = (x[:, :CA] + total_a).astype(BF)
        out[t, :, CA:] = (x[:, CA:] + total_b).astype(BF)

        @pl.when(jnp.logical_and(s < N - 1, t < N - 1))
        def _():
            hop_copy(t).start()

        for phase in range(8):
            sent(phase)
        return carry

    lax.fori_loop(0, N, tick, 0)

    @pl.when(s < N - 1)
    def _():
        for t in range(N - 1):
            hop_copy(t).wait_send()


def folded(rows):
    lead = rows.shape[:-2]
    count = rows.shape[-2]
    axes = tuple(range(len(lead))) + (len(lead) + 1, len(lead), len(lead) + 2)
    part_a = rows[..., :WA].reshape(lead + (count, 4, CA)).transpose(axes)
    part_b = rows[..., WA:].reshape(lead + (count, 4, CB)).transpose(axes)
    return jnp.concatenate([part_a, part_b], axis=-1).reshape(lead + (4 * count, CA + CB))


def unfolded(blocks):
    lead = blocks.shape[:-2]
    axes = tuple(range(len(lead))) + (len(lead) + 1, len(lead), len(lead) + 2)
    split = blocks.reshape(lead + (4, ROWS, CA + CB)).transpose(axes)
    return jnp.concatenate([split[..., :CA].reshape(lead + (ROWS, WA)),
                            split[..., CA:].reshape(lead + (ROWS, D - WA))], axis=-1)


def slot_weights(picked, weights):
    flat = picked.reshape(N, -1)
    order = jnp.arange(flat.shape[1])
    earlier = (flat[:, None, :] == flat[:, :, None]) & (order[None, None, :] < order[None, :, None])
    place = jnp.sum(earlier.astype(jnp.int32), axis=2).reshape(picked.shape)
    slot = picked * CAP + place
    hit = slot[..., None] == jnp.arange(N * CAP)
    return jnp.sum(jnp.where(hit, weights[..., None], 0.0), axis=2)


def body(micro_inputs, norm_gain, gate_up, down_proj, routes, route_weights):
    s = lax.axis_index("section")
    e = lax.axis_index("expert")
    z, y = e // N, e % N
    first = lax.dynamic_index_in_dim(micro_inputs, jnp.where(s == 0, 0, N - 1 + s), 0, keepdims=True)
    ent = folded(jnp.concatenate([first, micro_inputs[1:N]], axis=0))
    gain = folded(jnp.broadcast_to(norm_gain[0].astype(F32), (ROWS, D)))

    own = slot_weights(routes[0], route_weights[0])
    every = lax.all_gather(own, "expert").reshape(N, N, N, ROWS, N, CAP)
    eye8 = jnp.eye(N, dtype=BF)
    eye4 = jnp.eye(4, dtype=BF)
    column = lax.dynamic_index_in_dim(every, y, 1, keepdims=False)
    hits_a = (lax.dynamic_index_in_dim(column, z, 3, keepdims=False) > 0).astype(BF)
    la = jnp.einsum("ztrc,zw,qp->tqzcwpr", hits_a, eye8, eye4).reshape(N, 64, 128)
    hits_b = (lax.dynamic_index_in_dim(every, z, 0, keepdims=False) > 0).astype(BF)
    lb = jnp.einsum("ytrec,yw,qp->teqycwpr", hits_b, eye8, eye4).reshape(N, 512, 128)
    mine = lax.dynamic_index_in_dim(every, z, 4, keepdims=False)
    wslot = jnp.sum(mine, axis=3).transpose(2, 1, 0, 3).reshape(N, 128, 1)
    wslot = jnp.broadcast_to(wslot, (N, 128, 128))
    index = np.arange(128)
    swapped = (index // 2 % 8) * 16 + index // 16 * 2 + index % 2
    perm = jnp.asarray(swapped[:, None] == index[None, :], BF)

    vmem = pl.BlockSpec(memory_space=pltpu.VMEM)
    out = pl.pallas_call(
        kernel,
        out_shape=jax.ShapeDtypeStruct((N, 16, CA + CB), BF),
        in_specs=[vmem] * 10,
        out_specs=vmem,
        scratch_shapes=[
            pltpu.VMEM((N, 16, CA + CB), BF),
            pltpu.VMEM((16, CA), BF), pltpu.VMEM((16, CB), BF),
            pltpu.VMEM((N, 16, CA), BF), pltpu.VMEM((N, 16, CB), BF),
            pltpu.VMEM((64, CA), BF), pltpu.VMEM((N, 64, CB), BF),
            pltpu.VMEM((N, 64, CA), BF), pltpu.VMEM((N, 64, CB), BF),
            pltpu.VMEM((N, 64, CA), BF), pltpu.VMEM((N, 64, CB), BF),
            pltpu.VMEM((N, 64, CA), BF), pltpu.VMEM((N, 64, CB), BF),
            pltpu.VMEM((N, 16, CA), BF), pltpu.VMEM((N, 16, CB), BF),
            pltpu.VMEM((N, 16, CA), BF), pltpu.VMEM((N, 16, CB), BF),
            pltpu.SemaphoreType.DMA((8, N)), pltpu.SemaphoreType.DMA((8, N)),
            pltpu.SemaphoreType.DMA((N,)), pltpu.SemaphoreType.DMA((N,)),
        ],
        compiler_params=pltpu.CompilerParams(
            collective_id=0, has_side_effects=True, vmem_limit_bytes=40 << 20),
    )(ent, gain, gate_up[0, 0], down_proj[0, 0], la, la.transpose(0, 2, 1), lb,
      lb.transpose(0, 2, 1), wslot, perm)
    return unfolded(out)[None]


def solution(mesh):
    return jax.shard_map(
        body,
        mesh=mesh,
        in_specs=(
            P(None, "expert", None),
            P("section", None),
            P("section", "expert", None, None),
            P("section", "expert", None, None),
            P("section", None, "expert", None),
            P("section", None, "expert", None),
        ),
        out_specs=P("section", None, "expert", None),
        check_vma=False,
    )
```

time: 675 us -> 437 us (0.65)
  the two profiles are of different devices: /device:TPU:8 before, /device:TPU:2 now
where the time goes in v1:
time: 437 us; the launch traced here: 436 us
  Pallas kernels  323 us (74%)
  blocking collectives  57.4 us (13%)
  local copies, waits for them, and re-layouts  40.9 us (9%)
  other arithmetic  14.1 us (3%)
    pallas_call x1, Pallas kernels, body(): pl.pallas_call(kernel, out_shape=jax.ShapeDtypeStruct((N, 16, CA + CB), B...  323 us
    all_gather x1, blocking collectives, body(): every = lax.all_gather(own, 'expert').reshape(N, N, N, ROWS, N, CAP)  57.4 us
    reshape x2, local copies, waits for them, and re-layouts, body(): jnp.einsum('ytrec,yw,qp->teqycwpr', hits_b, eye8, eye4).reshape(N, 512, 128)  29.4 us

profile of v1, /device:TPU:2, one launch (start us, length us, event | category | flops | bytes accessed | tf_op | source)
XLA Modules:
  0.0 435.9 jit_solution(9165536188334872601)
XLA Ops:
  0.0 0.8 copy.57
  0.8 0.3 convert_reduce_fusion
  1.1 0.1 copy.59
  1.1 0.7 broadcast_multiply_fusion.2
  1.8 0.7 convert_reduce_fusion.2
  2.6 0.7 convert_reduce_fusion.1
  3.3 0.8 select_reduce_fusion
  4.2 0.8 constant_dynamic-slice_fusion
  5.0 0.1 multiply_bitcast_fusion
  5.0 1.0 slice.32
  6.1 0.1 fusion.1
  6.2 0.1 pad_maximum_fusion
  6.3 0.1 reshape.100.ent
  6.4 57.4 %all-gather = f32[512,4,16]{2,1,0:T(4,128)S(1)} all-gather(f32[8,4,16]{2,1,0:T(4,128)S(1)} %copy.64), channel_id=2, replica_groups=mesh['section'=8,'expert'=64] {'expert'}, dimensions={0}, use_global_device_ids=true | all-gather | bytes 133120 | tf_op jit(solution)/shard_map/all_gather | solution.py:219
  63.7 0.3 copy.65
  64.1 1.1 reshape.103
  65.2 0.1 compare_convert_fusion
  65.4 0.1 copy.68
  65.5 0.1 copy.70
  65.6 0.2 broadcast_in_dim.39.wslot
  65.8 1.3 broadcast_multiply_fusion.1
  67.1 0.9 copy.72.la
  68.0 2.4 copy.67
  70.4 8.4 %broadcast_multiply_fusion = bf16[8,4,4,8,8,4,8,2]{4,5,2,3,7,0,1,6:T(4,128)(2,1)} fusion(bf16[8,8,4,8,2]{1,2,4,0,3:T(4,128)(2,1)S(1)} %copy.68, bf16[8,4,4,8]{2,3,0,1:T(8,128)(2,1)S(1)} %multiply_bitcast_fusion), kind=kLoop, calls=%fused_computation | loop fusion | flops 524288 | bytes 1058816 | tf_op jit(solution)/shard_map/ytrec,yw,qp->teqycwpr/dot_general | solution.py:226
  78.8 12.4 %copy.73.lb = bf16[8,512,128]{2,1,0:T(8,128)(2,1)S(1)} copy(bf16[8,512,128]{0,2,1:T(8,128)(2,1)} %bitcast.41) | data formatting | bytes 2097152 | tf_op jit(solution)/shard_map/reshape | solution.py:226
  91.2 17.0 %copy.69 = bf16[8,512,128]{1,2,0:T(8,128)(2,1)S(1)} copy(bf16[8,512,128]{0,2,1:T(8,128)(2,1)} %bitcast.42) | data formatting | bytes 2097152 | tf_op jit(solution)/shard_map/reshape | solution.py:226
  108.2 1.5 copy-done
  109.7 1.2 copy-done.1
  110.9 0.8 copy-done.2
  111.6 323.3 %shard_map.73 = bf16[8,16,896]{2,1,0:T(8,128)(2,1)S(1)} custom-call(bf16[8,16,896]{2,1,0:T(8,128)(2,1)S(1)} %reshape.100.ent, f32[16,896]{1,0:T(8,128)S(1)} %reshape.101.gain, bf16[3584,256]{1,0:T(8,128)(2,1)S(1)} %bitcast.38, bf16[128,3584]{1,0:T(8,128)(2,1)S(1)} %bitcast.40, bf16[8,64,128]{2,1,0:T(8,128)(2,1)S(1)} %copy.72.la, ...), custom_call_target="tpu_custom_call" | custom-call | tf_op jit(solution)/shard_map/pallas_call | solution.py:235
  434.9 0.1 reshape.108
  435.1 0.8 maximum_bitcast_fusion
  (22 shorter events, 0.4 us)
Async XLA Ops:
  108.2 1.5 copy-start
  109.7 1.2 copy-start.1
  110.9 0.8 copy-start.2

commit v2 on v1

v2 whole, which is shorter than its diff:
```python
import numpy as np
import jax
import jax.numpy as jnp
from jax import lax
from jax.experimental import pallas as pl
from jax.experimental.pallas import tpu as pltpu
from jax.sharding import PartitionSpec as P

D = 3584
FF = 128
N = 8
ROWS = 4
CAP = 2
CA = 512
CB = 384
WA = 4 * CA
NB = 2
G = N // NB
SL = G * CAP
GR = G * 16
BLK = 4 * SL
EPSILON = 1e-06
MESH = pl.DeviceIdType.MESH
ORDER = (4, 3, 5, 2, 6, 1, 7)
BF = jnp.bfloat16
F32 = jnp.float32


def dot(a, b):
    return jnp.dot(a, b, preferred_element_type=F32)


def dot_t(a, b):
    return lax.dot_general(a, b, (((1,), (1,)), ((), ())), preferred_element_type=F32)


def exact(a, b):
    return jnp.dot(a, b, preferred_element_type=F32, precision=lax.Precision.HIGHEST)


def kernel(ent, gain, hown, wg_hbm, wd_hbm, e1, gt, mt, ma, mb, perm, sw, out,
           wg, wd, hop, hz, hy, hzt, hyt, wsend, wbuf, la, lb, ra, rb,
           na, nb, sa, sb, ba_send, bb_send, ba, bb, pa_send, pb_send, pa, pb,
           qa_send, qb_send, qa, qb, ssem, rsem, s1, r1, hs, hr, wsem):
    s = lax.axis_index("section")
    e = lax.axis_index("expert")
    z, y = e // N, e % N
    mine = (z + y) % NB

    def on_z(d):
        return (s, ((z + d) % N) * N + y)

    def on_y(d):
        return (s, z * N + (y + d) % N)

    load_g = pltpu.make_async_copy(wg_hbm.at[0, 0], wg, wsem.at[0])
    load_d = pltpu.make_async_copy(wd_hbm.at[0, 0], wd, wsem.at[1])
    load_g.start()
    load_d.start()

    bar = pltpu.get_barrier_semaphore()
    for d in range(1, N):
        pl.semaphore_signal(bar, inc=1, device_id=on_z(d), device_id_type=MESH)
        pl.semaphore_signal(bar, inc=1, device_id=on_y(d), device_id_type=MESH)
    pl.semaphore_signal(bar, inc=1, device_id=((s + 1) % N, e), device_id_type=MESH)
    pl.semaphore_signal(bar, inc=1, device_id=((s + N - 1) % N, e), device_id_type=MESH)
    pl.semaphore_wait(bar, 2 * (N - 1) + 2)

    def remote(phase, h, d, src, dst, target):
        return pltpu.make_async_remote_copy(
            src_ref=src, dst_ref=dst, send_sem=ssem.at[phase, h, d], recv_sem=rsem.at[phase, h, d],
            device_id=target, device_id_type=MESH)

    def once(phase, d, src, dst, target):
        return pltpu.make_async_remote_copy(
            src_ref=src, dst_ref=dst, send_sem=s1.at[phase, d], recv_sem=r1.at[phase, d],
            device_id=target, device_id_type=MESH)

    def at(v):
        return (v % NB) * G + v // NB

    def table_copies(d, back):
        zz, yy = ((z + N - d) % N, (y + N - d) % N) if back else (z, y)
        return (once(0, d, hown, hz.at[at(zz)], on_z(d)), once(1, d, hown, hy.at[at(yy)], on_y(d)))

    def weight_copy(d, back):
        return once(2, d, wsend, wbuf.at[(y + N - d) % N if back else y], on_y(d))

    def small_a(h, d, back):
        return remote(0, h, d, na, sa.at[h, ((z + N - d) % N if back else z) // NB], on_z(d))

    def small_b(h, d, back):
        return remote(1, h, d, nb, sb.at[h, ((y + N - d) % N if back else y) // NB], on_y(d))

    def big_a(h, d, back):
        return remote(2, h, d, ba_send.at[h], ba.at[h, (y + N - d) % N if back else y], on_y(d))

    def big_b(h, d, back):
        return remote(3, h, d, bb_send.at[h, (z + d) % N], bb.at[h, (z + N - d) % N if back else z],
                      on_z(d))

    def ret_a(h, d, back):
        return remote(4, h, d, pa_send.at[h, (y + d) % N], pa.at[h, (y + N - d) % N if back else y],
                      on_y(d))

    def ret_b(h, d, back):
        return remote(5, h, d, pb_send.at[h, (z + d) % N], pb.at[h, (z + N - d) % N if back else z],
                      on_z(d))

    def home_a(h, d, back):
        return remote(6, h, d, qa_send.at[h, ((z + d) % N) // NB],
                      qa.at[(z + N - d) % N if back else z], on_z(d))

    def home_b(h, d, back):
        return remote(7, h, d, qb_send.at[h, ((y + d) % N) // NB],
                      qb.at[(y + N - d) % N if back else y], on_y(d))

    def hop_copy(t):
        return pltpu.make_async_remote_copy(
            src_ref=out.at[t], dst_ref=hop.at[t + 1], send_sem=hs.at[t], recv_sem=hr.at[t],
            device_id=((s + 1) % N, e), device_id_type=MESH)

    def each_source(h, act):
        first = (mine + NB - h) % NB
        for k in range(G - 1, 0, -1):
            act(k * NB + first)

        @pl.when(first != 0)
        def _():
            act(first)

    def each_home(h, act):
        first = (h + NB - mine) % NB
        for k in range(G - 1, 0, -1):
            act(k * NB + first)

        @pl.when(first != 0)
        def _():
            act(first)

    def spread_hits(h, t):
        from_z = pl.multiple_of(((h + N - y) % NB) * (G * 8), G * 8)
        from_y = pl.multiple_of(((h + N - z) % NB) * (G * 8), G * 8)
        xz = dot(e1[...], hzt[t, pl.ds(from_z, G * 8), :]).astype(BF)
        xy = dot(e1[...], hyt[t, pl.ds(from_y, G * 8), :]).astype(BF)
        return xz, xy, gt[pl.ds(pl.multiple_of(z * BLK, BLK), BLK), :]

    def begin(h, t):
        @pl.when(mine == h)
        def _():
            @pl.when(jnp.logical_or(s == 0, t == 0))
            def _():
                out[t] = ent[t]

            @pl.when(jnp.logical_and(s > 0, t > 0))
            def _():
                hop_copy(t - 1).wait_recv()
                out[t] = hop[t]

            x = out[t].astype(F32)
            ss = jnp.sum(x * x, axis=1, keepdims=True)
            ss = ss + pltpu.roll(ss, 8, 0)
            ss = ss + pltpu.roll(ss, 4, 0)
            n = ((x * lax.rsqrt(ss * (1.0 / D) + EPSILON)) * gain[...]).astype(BF)
            na[...] = n[:, :CA]
            nb[...] = n[:, CA:]
            for d in ORDER:
                small_a(h, d, False).start()
                small_b(h, d, False).start()
            sa[h, z // NB] = n[:, :CA]
            sb[h, y // NB] = n[:, CA:]

        if h == 0:
            @pl.when(t == 0)
            def _():
                for d in ORDER:
                    for c in table_copies(d, True):
                        c.wait_recv()
                all_z = hz[...].reshape(64, 128)
                all_y = hy[...].reshape(64, 128)
                for i in range(N):
                    hzt[i] = jnp.where(pltpu.roll(all_z, (128 - 16 * i) % 128, 1) > 0, 1.0, 0.0).astype(BF)
                    hyt[i] = jnp.where(pltpu.roll(all_y, (128 - 16 * i) % 128, 1) > 0, 1.0, 0.0).astype(BF)
                lane = lax.broadcasted_iota(jnp.int32, (128, 128), 0)
                tick_of = lax.broadcasted_iota(jnp.int32, (128, 128), 1)
                pick = jnp.where((lane // 16 == tick_of) & ((lane // 2) % N == z), 1.0, 0.0)
                odd = lax.broadcasted_iota(jnp.int32, (SL, 128), 1) % 2
                row = lax.broadcasted_iota(jnp.int32, (SL, 128), 0) % 2
                for g in range(NB):
                    sums = exact(sw[...], hz[pl.ds(((g + N - y) % NB) * G, G)].reshape(G * 8, 128))
                    wsend[g * SL:(g + 1) * SL, :] = exact(jnp.where(odd == row, sums, 0.0), pick)
                for d in ORDER:
                    weight_copy(d, False).start()
                wbuf[y] = wsend[...]

        xz, xy, gz = spread_hits(h, t)
        la[h] = (dot_t(gz, xz) * mt[...]).astype(BF)
        lb[h] = (dot_t(gt[...], xy).reshape(N, BLK, GR) * mt[...][None]).reshape(N * BLK, GR).astype(BF)

    def select(h, t):
        each_source(h, lambda d: small_a(h, d, True).wait_recv())
        ba_send[h] = dot(la[h], sa[h].reshape(GR, CA)).astype(BF)
        for d in ORDER:
            big_a(h, d, False).start()
        ba[h, y] = ba_send[h]
        each_source(h, lambda d: small_b(h, d, True).wait_recv())
        bb_send[h] = dot(lb[h], sb[h].reshape(GR, CB)).astype(BF).reshape(N, BLK, CB)
        for d in ORDER:
            big_b(h, d, False).start()
        bb[h, z] = bb_send[h, z]

    def quarter(block, q, columns):
        return block[:, SL * q:SL * q + SL, :].reshape(N * SL, columns).astype(BF)

    def outward(rows, first, columns):
        parts = [dot(rows, wd[:, first + q * columns:first + (q + 1) * columns]).reshape(N, SL, columns)
                 for q in range(4)]
        return jnp.concatenate(parts, axis=1).astype(BF)

    def experts(h, t):
        if h == 0:
            @pl.when(t == 0)
            def _():
                load_g.wait()
                load_d.wait()
                for d in ORDER:
                    weight_copy(d, True).wait_recv()
        for d in ORDER:
            big_b(h, d, True).wait_recv()
        rows_b = bb[h].astype(F32)
        proj_b = jnp.zeros((N * SL, 2 * FF), F32)
        for q in range(4):
            proj_b += dot(quarter(rows_b, q, CB), wg[WA + q * CB:WA + (q + 1) * CB, :])
        high = proj_b.astype(BF)
        low = (proj_b - high.astype(F32)).astype(BF)
        proj = dot(perm[h], high) + dot(perm[h], low)
        tick_lane = lax.broadcasted_iota(jnp.int32, (N * SL, 128), 1) == t
        weight = jnp.sum(jnp.where(tick_lane, wbuf[:, SL * h:SL * h + SL, :].reshape(N * SL, 128), 0.0),
                         axis=1, keepdims=True)
        for d in ORDER:
            big_a(h, d, True).wait_recv()
        rows_a = ba[h].astype(F32)
        for q in range(4):
            proj += dot(quarter(rows_a, q, CA), wg[q * CA:(q + 1) * CA, :])
        gate, up = proj[:, :FF], proj[:, FF:]
        inner = (gate / (1.0 + jnp.exp(-gate)) * up * weight).astype(BF)
        pa_send[h] = outward(inner, 0, CA)
        for d in ORDER:
            ret_a(h, d, False).start()
        pb_send[h] = outward(dot(perm[h], inner).astype(BF), WA, CB)
        for d in ORDER:
            ret_b(h, d, False).start()
        pa[h, y] = pa_send[h, y]
        pb[h, z] = pb_send[h, z]
        xz, xy, gz = spread_hits(h, t)
        ra[h] = (dot_t(xz, gz) * ma[...]).astype(BF)
        rb[h] = (dot_t(xy, gt[...]) * mb[...]).astype(BF)

        @pl.when(mine == h)
        def _():
            for d in ORDER:
                small_a(h, d, False).wait_send()
                small_b(h, d, False).wait_send()

    def gather(h, t):
        @pl.when(t > 0)
        def _():
            each_home(h, lambda d: (home_a(h, d, False).wait_send(), home_b(h, d, False).wait_send()))
        for d in ORDER:
            ret_b(h, d, True).wait_recv()
        qb_send[h] = dot(rb[h], pb[h].reshape(N * BLK, CB)).astype(BF).reshape(G, 16, CB)
        each_home(h, lambda d: home_b(h, d, False).start())
        for d in ORDER:
            ret_a(h, d, True).wait_recv()
        total = pa[h, 0].astype(F32)
        for i in range(1, N):
            total += pa[h, i].astype(F32)
        qa_send[h] = dot(ra[h], total.astype(BF)).astype(BF).reshape(G, 16, CA)
        each_home(h, lambda d: home_a(h, d, False).start())
        for d in ORDER:
            big_a(h, d, False).wait_send()
            big_b(h, d, False).wait_send()
            ret_a(h, d, False).wait_send()
            ret_b(h, d, False).wait_send()

    def finish(h, t):
        @pl.when(mine == h)
        def _():
            qa[z] = qa_send[h, z // NB]
            qb[y] = qb_send[h, y // NB]
            x = out[t].astype(F32)
            for d in ORDER:
                home_b(h, d, True).wait_recv()
            total_b = qb[0].astype(F32)
            for i in range(1, N):
                total_b += qb[i].astype(F32)
            for d in ORDER:
                home_a(h, d, True).wait_recv()
            total_a = qa[0].astype(F32)
            for i in range(1, N):
                total_a += qa[i].astype(F32)
            out[t, :, :CA] = (x[:, :CA] + total_a).astype(BF)
            out[t, :, CA:] = (x[:, CA:] + total_b).astype(BF)

            @pl.when(jnp.logical_and(s < N - 1, t < N - 1))
            def _():
                hop_copy(t).start()

    for d in ORDER:
        for c in table_copies(d, False):
            c.start()
    hz[at(z)] = hown[...]
    hy[at(y)] = hown[...]

    if NB == 1:
        def tick(t, carry):
            for stage in (begin, select, experts, gather, finish):
                stage(0, t)
            return carry

        lax.fori_loop(0, N, tick, 0)
    else:
        def tick(t, carry):
            @pl.when(t < N)
            def _():
                begin(0, t)
                select(0, t)

            @pl.when(t > 0)
            def _():
                gather(1, t - 1)
                finish(1, t - 1)

            @pl.when(t < N)
            def _():
                experts(0, t)
                begin(1, t)
                select(1, t)
                gather(0, t)
                finish(0, t)
                experts(1, t)
            return carry

        lax.fori_loop(0, N + 1, tick, 0)

    for h in range(NB):
        each_home(h, lambda d: (home_a(h, d, False).wait_send(), home_b(h, d, False).wait_send()))
    for d in ORDER:
        for c in table_copies(d, False):
            c.wait_send()
        weight_copy(d, False).wait_send()

    @pl.when(s < N - 1)
    def _():
        for t in range(N - 1):
            hop_copy(t).wait_send()


def folded(rows):
    lead = rows.shape[:-2]
    count = rows.shape[-2]
    axes = tuple(range(len(lead))) + (len(lead) + 1, len(lead), len(lead) + 2)
    part_a = rows[..., :WA].reshape(lead + (count, 4, CA)).transpose(axes)
    part_b = rows[..., WA:].reshape(lead + (count, 4, CB)).transpose(axes)
    return jnp.concatenate([part_a, part_b], axis=-1).reshape(lead + (4 * count, CA + CB))


def unfolded(blocks):
    lead = blocks.shape[:-2]
    axes = tuple(range(len(lead))) + (len(lead) + 1, len(lead), len(lead) + 2)
    split = blocks.reshape(lead + (4, ROWS, CA + CB)).transpose(axes)
    return jnp.concatenate([split[..., :CA].reshape(lead + (ROWS, WA)),
                            split[..., CA:].reshape(lead + (ROWS, D - WA))], axis=-1)


def slot_weights(picked, weights):
    flat = picked.reshape(N, -1)
    order = jnp.arange(flat.shape[1])
    earlier = (flat[:, None, :] == flat[:, :, None]) & (order[None, None, :] < order[None, :, None])
    place = jnp.sum(earlier.astype(jnp.int32), axis=2).reshape(picked.shape)
    slot = picked * CAP + place
    hit = slot[..., None] == jnp.arange(N * CAP)
    return jnp.sum(jnp.where(hit, weights[..., None], 0.0), axis=2)


def constants():
    e1 = np.zeros((G, 4, ROWS, G, 8), np.float32)
    for i in range(G):
        for r in range(ROWS):
            e1[i, :, r, i, r] = 1
    gt = np.zeros((N, 4, G, CAP, 128), np.float32)
    for k in range(N):
        for c in range(CAP):
            gt[k, :, :, c, k * CAP + c] = 1
    mt = np.zeros((4, G, CAP, G, 4, ROWS), np.float32)
    for q in range(4):
        for i in range(G):
            mt[q, i, :, i, q, :] = 1
    mt = mt.reshape(BLK, GR)
    sw = np.zeros((G, CAP, G, 8), np.float32)
    for i in range(G):
        sw[i, :, i, :ROWS] = 1
    perm = np.zeros((NB, N * SL, N * SL), np.float32)
    for k in range(N):
        for j in range(N):
            for c in range(CAP):
                perm[(k + j) % NB, j * SL + k // NB * CAP + c, k * SL + j // NB * CAP + c] = 1
    return (jnp.asarray(e1.reshape(GR, G * 8), BF), jnp.asarray(gt.reshape(N * BLK, 128), BF),
            jnp.asarray(mt), jnp.asarray(mt.T), jnp.asarray(np.tile(mt.T, (1, N))),
            jnp.asarray(perm, BF), jnp.asarray(sw.reshape(SL, G * 8)))


def body(micro_inputs, norm_gain, gate_up, down_proj, routes, route_weights):
    s = lax.axis_index("section")
    first = lax.dynamic_index_in_dim(micro_inputs, jnp.where(s == 0, 0, N - 1 + s), 0, keepdims=True)
    ent = folded(jnp.concatenate([first, micro_inputs[1:N]], axis=0))
    gain = folded(jnp.broadcast_to(norm_gain[0].astype(F32), (ROWS, D)))
    own = slot_weights(routes[0], route_weights[0]).transpose(1, 0, 2).reshape(ROWS, 128)
    own = jnp.concatenate([own, jnp.zeros_like(own)], axis=0)

    vmem = pl.BlockSpec(memory_space=pltpu.VMEM)
    hbm = pl.BlockSpec(memory_space=pl.ANY)
    out = pl.pallas_call(
        kernel,
        out_shape=jax.ShapeDtypeStruct((N, 16, CA + CB), BF),
        in_specs=[vmem] * 3 + [hbm] * 2 + [vmem] * 7,
        out_specs=vmem,
        scratch_shapes=[
            pltpu.VMEM((D, 2 * FF), BF), pltpu.VMEM((FF, D), BF),
            pltpu.VMEM((N, 16, CA + CB), BF),
            pltpu.VMEM((N, 8, 128), F32), pltpu.VMEM((N, 8, 128), F32),
            pltpu.VMEM((N, 64, 128), BF), pltpu.VMEM((N, 64, 128), BF),
            pltpu.VMEM((16, 128), F32), pltpu.VMEM((N, 16, 128), F32),
            pltpu.VMEM((NB, BLK, GR), BF), pltpu.VMEM((NB, N * BLK, GR), BF),
            pltpu.VMEM((NB, GR, BLK), BF), pltpu.VMEM((NB, GR, N * BLK), BF),
            pltpu.VMEM((16, CA), BF), pltpu.VMEM((16, CB), BF),
            pltpu.VMEM((NB, G, 16, CA), BF), pltpu.VMEM((NB, G, 16, CB), BF),
            pltpu.VMEM((NB, BLK, CA), BF), pltpu.VMEM((NB, N, BLK, CB), BF),
            pltpu.VMEM((NB, N, BLK, CA), BF), pltpu.VMEM((NB, N, BLK, CB), BF),
            pltpu.VMEM((NB, N, BLK, CA), BF), pltpu.VMEM((NB, N, BLK, CB), BF),
            pltpu.VMEM((NB, N, BLK, CA), BF), pltpu.VMEM((NB, N, BLK, CB), BF),
            pltpu.VMEM((NB, G, 16, CA), BF), pltpu.VMEM((NB, G, 16, CB), BF),
            pltpu.VMEM((N, 16, CA), BF), pltpu.VMEM((N, 16, CB), BF),
            pltpu.SemaphoreType.DMA((8, NB, N)), pltpu.SemaphoreType.DMA((8, NB, N)),
            pltpu.SemaphoreType.DMA((3, N)), pltpu.SemaphoreType.DMA((3, N)),
            pltpu.SemaphoreType.DMA((N,)), pltpu.SemaphoreType.DMA((N,)),
            pltpu.SemaphoreType.DMA((2,)),
        ],
        compiler_params=pltpu.CompilerParams(
            collective_id=0, has_side_effects=True, vmem_limit_bytes=40 << 20),
    )(ent, gain, own, gate_up, down_proj, *constants())
    return unfolded(out)[None]


def solution(mesh):
    return jax.shard_map(
        body,
        mesh=mesh,
        in_specs=(
            P(None, "expert", None),
            P("section", None),
            P("section", "expert", None, None),
            P("section", "expert", None, None),
            P("section", None, "expert", None),
            P("section", None, "expert", None),
        ),
        out_specs=P("section", None, "expert", None),
        check_vma=False,
    )
```

time: 437 us -> 324 us (0.74)
  the two profiles are of different devices: /device:TPU:2 before, /device:TPU:14 now
where the time goes in v2:
time: 324 us; the launch traced here: 323 us
  Pallas kernels  315 us (97%)
  local copies, waits for them, and re-layouts  4.3 us (1%)
  other arithmetic  4.24 us (1%)
    pallas_call x1, Pallas kernels, body(): pl.pallas_call(kernel, out_shape=jax.ShapeDtypeStruct((N, 16, CA + CB), B...  315 us

profile of v2, /device:TPU:14, one launch (start us, length us, event | category | flops | bytes accessed | tf_op | source)
XLA Modules:
  0.0 323.4 jit_solution(14500489244578987768)
XLA Ops:
  0.0 0.0 copy-start.8
  0.0 0.0 copy-start.5
  0.0 0.0 copy-start.6
  0.0 0.0 copy-start.3
  0.0 0.0 copy-start.7
  0.1 0.0 copy-start
  0.1 0.9 copy.26
  1.0 0.3 convert_reduce_fusion
  1.3 0.1 copy.28
  1.3 0.7 broadcast_multiply_fusion
  2.1 0.7 convert_reduce_fusion.2
  2.8 0.7 convert_reduce_fusion.1
  3.5 0.8 select_reduce_fusion
  4.3 0.1 reshape.81
  4.5 0.8 constant_dynamic-slice_fusion
  5.2 1.0 slice.32
  6.3 0.1 fusion
  6.4 0.1 pad_maximum_fusion
  6.5 0.1 reshape.78.ent
  6.6 0.0 copy-done.8
  6.6 0.0 copy-done.4
  6.6 0.0 copy-done.2
  6.6 0.0 copy-done.5
  6.6 0.0 copy-done.6
  6.6 0.0 copy-done.3
  6.6 0.0 copy-done.7
  6.6 0.0 copy-done
  6.6 0.0 copy-start.1
  6.7 1.2 copy-done.1
  7.8 314.6 %shard_map.127 = bf16[8,16,896]{2,1,0:T(8,128)(2,1)S(1)} custom-call(bf16[8,16,896]{2,1,0:T(8,128)(2,1)S(1)} %reshape.78.ent, f32[16,896]{1,0:T(8,128)S(1)} %reshape.79.gain, f32[8,128]{1,0:T(8,128)S(1)} %concatenate.18.hown, bf16[1,1,3584,256]{3,2,1,0:T(8,128)(2,1)S(1)} %copy-done, bf16[1,1,128,3584]{3,2,1,0:T(8,128)(2,1)S(1)} %copy-done.1, ...), custom_call_target="tpu_custom_call" | custom-call | tf_op jit(solution)/shard_map/pallas_call | solution.py:423
  322.5 0.1 reshape.82
  322.6 0.8 maximum_bitcast_fusion
  (15 shorter events, 0.2 us)
Async XLA Ops:
  0.0 6.6 %copy-start.8 = (f32[8,32]{1,0:T(8,128)S(1)}, f32[8,32]{1,0:T(8,128)}, u32[]{:S(2)}) copy-start(f32[8,32]{1,0:T(8,128)} %constant.40.clone.sw) | copy-start | bytes 3076
  0.0 6.6 %copy-start.4 = (bf16[2,64,64]{2,1,0:T(8,128)(2,1)S(1)}, bf16[2,64,64]{2,1,0:T(8,128)(2,1)}, u32[]{:S(2)}) copy-start(bf16[2,64,64]{2,1,0:T(8,128)(2,1)} %constant.39.clone.perm) | copy-start | bytes 49156
  0.0 6.6 %copy-start.2 = (f32[64,256]{1,0:T(8,128)S(1)}, f32[64,256]{1,0:T(8,128)}, u32[]{:S(2)}) copy-start(f32[64,256]{1,0:T(8,128)} %constant.38.clone.mb) | copy-start | bytes 196612
  0.0 6.6 %copy-start.5 = (f32[64,32]{1,0:T(8,128)S(1)}, f32[64,32]{1,0:T(8,128)}, u32[]{:S(2)}) copy-start(f32[64,32]{1,0:T(8,128)} %constant.37.clone.ma) | copy-start | bytes 24580
  0.0 6.6 %copy-start.6 = (f32[32,64]{1,0:T(8,128)S(1)}, f32[32,64]{1,0:T(8,128)}, u32[]{:S(2)}) copy-start(f32[32,64]{1,0:T(8,128)} %constant.36.clone.mt) | copy-start | bytes 24580
  0.0 6.6 %copy-start.3 = (bf16[256,128]{1,0:T(8,128)(2,1)S(1)}, bf16[256,128]{1,0:T(8,128)(2,1)}, u32[]{:S(2)}) copy-start(bf16[256,128]{1,0:T(8,128)(2,1)} %constant.35.clone.gt) | copy-start | bytes 196612
  0.0 6.6 %copy-start.7 = (bf16[64,32]{1,0:T(8,128)(2,1)S(1)}, bf16[64,32]{1,0:T(8,128)(2,1)}, u32[]{:S(2)}) copy-start(bf16[64,32]{1,0:T(8,128)(2,1)} %constant.34.clone.e1) | copy-start | bytes 12292
  0.1 6.6 %copy-start = (bf16[1,1,3584,256]{3,2,1,0:T(8,128)(2,1)S(1)}, bf16[1,1,3584,256]{3,2,1,0:T(8,128)(2,1)}, u32[]{:S(2)}) copy-start(bf16[1,1,3584,256]{3,2,1,0:T(8,128)(2,1)} %wg_hbm.1) | copy-start | bytes 5505028
  6.6 1.2 copy-start.1

commit v3 on v2

--- a/solution.py
+++ b/solution.py
@@ -38,8 +38,14 @@
     return jnp.dot(a, b, preferred_element_type=F32, precision=lax.Precision.HIGHEST)
 
 
-def kernel(ent, gain, hown, wg_hbm, wd_hbm, e1, gt, mt, ma, mb, perm, sw, out,
-           wg, wd, hop, hz, hy, hzt, hyt, wsend, wbuf, la, lb, ra, rb,
+def folded(x):
+    part_a = jnp.concatenate([x[:, q * CA:(q + 1) * CA] for q in range(4)], axis=0)
+    part_b = jnp.concatenate([x[:, WA + q * CB:WA + (q + 1) * CB] for q in range(4)], axis=0)
+    return jnp.concatenate([part_a, part_b], axis=1)
+
+
+def kernel(micro, norm_gain, picked, weights, wg_hbm, wd_hbm, e1, gt, mt, ma, mb, perm, sw, out,
+           gain, hown, wg, wd, hop, hz, hy, hzt, hyt, wsend, wbuf, la, lb, ra, rb,
            na, nb, sa, sb, ba_send, bb_send, ba, bb, pa_send, pb_send, pa, pb,
            qa_send, qb_send, qa, qb, ssem, rsem, s1, r1, hs, hr, wsem):
     s = lax.axis_index("section")
@@ -57,6 +63,18 @@
     load_d = pltpu.make_async_copy(wd_hbm.at[0, 0], wd, wsem.at[1])
     load_g.start()
     load_d.start()
+
+    gain[...] = folded(jnp.broadcast_to(norm_gain[...].astype(F32), (ROWS, D)))
+    lanes = lax.broadcasted_iota(jnp.int32, (8, 128), 1)
+    row = lax.broadcasted_iota(jnp.int32, (8, 128), 0)
+    expert = (lanes >> 1) & 7
+    first_pick, second_pick = picked[0] == expert, picked[1] == expert
+    taken = jnp.where(first_pick | second_pick, 1.0, 0.0)
+    ahead = jnp.zeros((8, 128), F32)
+    for i in range(1, ROWS):
+        ahead += jnp.where(row >= i, pltpu.roll(taken, i, 0), 0.0)
+    in_place = (ahead == (lanes & 1).astype(F32)) & (taken > 0)
+    hown[...] = jnp.where(in_place, jnp.where(first_pick, weights[0], weights[1]), 0.0)
 
     bar = pltpu.get_barrier_semaphore()
     for d in range(1, N):
@@ -150,7 +168,7 @@
         def _():
             @pl.when(jnp.logical_or(s == 0, t == 0))
             def _():
-                out[t] = ent[t]
+                out[t] = folded(micro[t + (s + N - 1) // N * (s + N - 1)].astype(F32)).astype(BF)
 
             @pl.when(jnp.logical_and(s > 0, t > 0))
             def _():
@@ -209,8 +227,14 @@
             big_b(h, d, False).start()
         bb[h, z] = bb_send[h, z]
 
-    def quarter(block, q, columns):
-        return block[:, SL * q:SL * q + SL, :].reshape(N * SL, columns).astype(BF)
+    def inward(block, first, columns):
+        per = 16 // SL
+        total = jnp.zeros((N * SL, 2 * FF), F32)
+        for q in range(4):
+            rows = block[:, q // per * 16:q // per * 16 + 16, :].reshape(N * 16, columns)
+            product = dot(rows, wg[first + q * columns:first + (q + 1) * columns, :])
+            total += product.reshape(N, per, SL, 2 * FF)[:, q % per].reshape(N * SL, 2 * FF)
+        return total
 
     def outward(rows, first, columns):
         parts = [dot(rows, wd[:, first + q * columns:first + (q + 1) * columns]).reshape(N, SL, columns)
@@ -227,10 +251,7 @@
                     weight_copy(d, True).wait_recv()
         for d in ORDER:
             big_b(h, d, True).wait_recv()
-        rows_b = bb[h].astype(F32)
-        proj_b = jnp.zeros((N * SL, 2 * FF), F32)
-        for q in range(4):
-            proj_b += dot(quarter(rows_b, q, CB), wg[WA + q * CB:WA + (q + 1) * CB, :])
+        proj_b = inward(bb[h], WA, CB)
         high = proj_b.astype(BF)
         low = (proj_b - high.astype(F32)).astype(BF)
         proj = dot(perm[h], high) + dot(perm[h], low)
@@ -239,9 +260,7 @@
                          axis=1, keepdims=True)
         for d in ORDER:
             big_a(h, d, True).wait_recv()
-        rows_a = ba[h].astype(F32)
-        for q in range(4):
-            proj += dot(quarter(rows_a, q, CA), wg[q * CA:(q + 1) * CA, :])
+        proj += inward(ba[h], 0, CA)
         gate, up = proj[:, :FF], proj[:, FF:]
         inner = (gate / (1.0 + jnp.exp(-gate)) * up * weight).astype(BF)
         pa_send[h] = outward(inner, 0, CA)
@@ -312,36 +331,17 @@
     hz[at(z)] = hown[...]
     hy[at(y)] = hown[...]
 
-    if NB == 1:
-        def tick(t, carry):
-            for stage in (begin, select, experts, gather, finish):
-                stage(0, t)
-            return carry
-
-        lax.fori_loop(0, N, tick, 0)
-    else:
-        def tick(t, carry):
-            @pl.when(t < N)
-            def _():
-                begin(0, t)
-                select(0, t)
-
-            @pl.when(t > 0)
-            def _():
-                gather(1, t - 1)
-                finish(1, t - 1)
-
-            @pl.when(t < N)
-            def _():
-                experts(0, t)
-                begin(1, t)
-                select(1, t)
-                gather(0, t)
-                finish(0, t)
-                experts(1, t)
-            return carry
-
-        lax.fori_loop(0, N + 1, tick, 0)
+    order = ((begin, 0, 0), (gather, 1, 1), (select, 0, 0), (finish, 1, 1), (begin, 1, 0),
+             (experts, 0, 0), (select, 1, 0), (gather, 0, 0), (experts, 1, 0), (finish, 0, 0))
+
+    def tick(t, carry):
+        for step, h, late in order:
+            @pl.when(t > 0 if late else t < N)
+            def _():
+                step(h, t - late)
+        return carry
+
+    lax.fori_loop(0, N + 1, tick, 0)
 
     for h in range(NB):
         each_home(h, lambda d: (home_a(h, d, False).wait_send(), home_b(h, d, False).wait_send()))
@@ -356,31 +356,12 @@
             hop_copy(t).wait_send()
 
 
-def folded(rows):
-    lead = rows.shape[:-2]
-    count = rows.shape[-2]
-    axes = tuple(range(len(lead))) + (len(lead) + 1, len(lead), len(lead) + 2)
-    part_a = rows[..., :WA].reshape(lead + (count, 4, CA)).transpose(axes)
-    part_b = rows[..., WA:].reshape(lead + (count, 4, CB)).transpose(axes)
-    return jnp.concatenate([part_a, part_b], axis=-1).reshape(lead + (4 * count, CA + CB))
-
-
 def unfolded(blocks):
     lead = blocks.shape[:-2]
     axes = tuple(range(len(lead))) + (len(lead) + 1, len(lead), len(lead) + 2)
     split = blocks.reshape(lead + (4, ROWS, CA + CB)).transpose(axes)
     return jnp.concatenate([split[..., :CA].reshape(lead + (ROWS, WA)),
                             split[..., CA:].reshape(lead + (ROWS, D - WA))], axis=-1)
-
-
-def slot_weights(picked, weights):
-    flat = picked.reshape(N, -1)
-    order = jnp.arange(flat.shape[1])
-    earlier = (flat[:, None, :] == flat[:, :, None]) & (order[None, None, :] < order[None, :, None])
-    place = jnp.sum(earlier.astype(jnp.int32), axis=2).reshape(picked.shape)
-    slot = picked * CAP + place
-    hit = slot[..., None] == jnp.arange(N * CAP)
-    return jnp.sum(jnp.where(hit, weights[..., None], 0.0), axis=2)
 
 
 def constants():
@@ -411,21 +392,19 @@
 
 
 def body(micro_inputs, norm_gain, gate_up, down_proj, routes, route_weights):
-    s = lax.axis_index("section")
-    first = lax.dynamic_index_in_dim(micro_inputs, jnp.where(s == 0, 0, N - 1 + s), 0, keepdims=True)
-    ent = folded(jnp.concatenate([first, micro_inputs[1:N]], axis=0))
-    gain = folded(jnp.broadcast_to(norm_gain[0].astype(F32), (ROWS, D)))
-    own = slot_weights(routes[0], route_weights[0]).transpose(1, 0, 2).reshape(ROWS, 128)
-    own = jnp.concatenate([own, jnp.zeros_like(own)], axis=0)
+    def spread(table, empty):
+        wide = jnp.repeat(table.transpose(2, 1, 0), 16, axis=2)
+        return jnp.concatenate([wide, jnp.full_like(wide, empty)], axis=1)
 
     vmem = pl.BlockSpec(memory_space=pltpu.VMEM)
     hbm = pl.BlockSpec(memory_space=pl.ANY)
     out = pl.pallas_call(
         kernel,
         out_shape=jax.ShapeDtypeStruct((N, 16, CA + CB), BF),
-        in_specs=[vmem] * 3 + [hbm] * 2 + [vmem] * 7,
+        in_specs=[vmem] * 4 + [hbm] * 2 + [vmem] * 7,
         out_specs=vmem,
         scratch_shapes=[
+            pltpu.VMEM((16, CA + CB), F32), pltpu.VMEM((8, 128), F32),
             pltpu.VMEM((D, 2 * FF), BF), pltpu.VMEM((FF, D), BF),
             pltpu.VMEM((N, 16, CA + CB), BF),
             pltpu.VMEM((N, 8, 128), F32), pltpu.VMEM((N, 8, 128), F32),
@@ -447,8 +426,9 @@
             pltpu.SemaphoreType.DMA((2,)),
         ],
         compiler_params=pltpu.CompilerParams(
-            collective_id=0, has_side_effects=True, vmem_limit_bytes=40 << 20),
-    )(ent, gain, own, gate_up, down_proj, *constants())
+            collective_id=0, has_side_effects=True, vmem_limit_bytes=56 << 20),
+    )(micro_inputs, norm_gain, spread(routes[0], -1), spread(route_weights[0], 0.0),
+      gate_up, down_proj, *constants())
     return unfolded(out)[None]
 
 

time: 324 us -> 289 us (0.89)
  the two profiles are of different devices: /device:TPU:14 before, /device:TPU:10 now
where the time goes in v3:
time: 289 us; the launch traced here: 288 us
  Pallas kernels  284 us (98%)
  local copies, waits for them, and re-layouts  3.99 us (1%)
    pallas_call x1, Pallas kernels, body(): pl.pallas_call(kernel, out_shape=jax.ShapeDtypeStruct((N, 16, CA + CB), B...  284 us

profile of v3, /device:TPU:10, one launch (start us, length us, event | category | flops | bytes accessed | tf_op | source)
XLA Modules:
  0.0 288.4 jit_solution(7422641654190806663)
XLA Ops:
  0.0 0.7 copy.19
  0.7 0.7 copy.18
  1.4 0.1 broadcast_in_dim.12
  1.5 0.1 reshape.16
  1.5 0.6 concatenate.10.weights
  2.1 0.1 broadcast_in_dim.11
  2.2 0.1 reshape.15
  2.3 0.6 concatenate.9.picked
  2.9 283.6 %shard_map.127 = bf16[8,16,896]{2,1,0:T(8,128)(2,1)} custom-call(bf16[15,4,3584]{2,1,0:T(4,128)(2,1)} %micro.1, bf16[1,3584]{1,0:T(2,128)(2,1)} %norm_gain.1, s32[2,8,128]{2,1,0:T(8,128)} %concatenate.9.picked, f32[2,8,128]{2,1,0:T(8,128)} %concatenate.10.weights, bf16[1,1,3584,256]{3,2,1,0:T(8,128)(2,1)} %wg_hbm.1, bf16[1,1,128,3584]{3,2,1,0:T(8,128)(2,1)} %wd_hbm.1, ...), custom_call_target="tpu_custom_call" | custom-call | tf_op jit(solution)/shard_map/pallas_call | solution.py:401
  286.5 1.0 reshape.17
  287.6 0.8 maximum_bitcast_fusion
  (2 shorter events, 0.1 us)

commit v4 on v3

--- a/solution.py
+++ b/solution.py
@@ -14,7 +14,7 @@
 CA = 512
 CB = 384
 WA = 4 * CA
-NB = 2
+NB = 4
 G = N // NB
 SL = G * CAP
 GR = G * 16
@@ -86,7 +86,7 @@
 
     def remote(phase, h, d, src, dst, target):
         return pltpu.make_async_remote_copy(
-            src_ref=src, dst_ref=dst, send_sem=ssem.at[phase, h, d], recv_sem=rsem.at[phase, h, d],
+            src_ref=src, dst_ref=dst, send_sem=ssem.at[phase, h], recv_sem=rsem.at[phase, h],
             device_id=target, device_id_type=MESH)
 
     def once(phase, d, src, dst, target):
@@ -104,48 +104,60 @@
     def weight_copy(d, back):
         return once(2, d, wsend, wbuf.at[(y + N - d) % N if back else y], on_y(d))
 
-    def small_a(h, d, back):
-        return remote(0, h, d, na, sa.at[h, ((z + N - d) % N if back else z) // NB], on_z(d))
-
-    def small_b(h, d, back):
-        return remote(1, h, d, nb, sb.at[h, ((y + N - d) % N if back else y) // NB], on_y(d))
-
-    def big_a(h, d, back):
-        return remote(2, h, d, ba_send.at[h], ba.at[h, (y + N - d) % N if back else y], on_y(d))
-
-    def big_b(h, d, back):
-        return remote(3, h, d, bb_send.at[h, (z + d) % N], bb.at[h, (z + N - d) % N if back else z],
+    def small_a(h, d):
+        return remote(0, h, d, na, sa.at[h, z // NB], on_z(d))
+
+    def small_b(h, d):
+        return remote(1, h, d, nb, sb.at[h, y // NB], on_y(d))
+
+    def big_a(h, d):
+        return remote(2, h, d, ba_send.at[h], ba.at[h, y], on_y(d))
+
+    def big_b(h, d):
+        return remote(3, h, d, bb_send.at[h, (z + d) % N], bb.at[h, z],
                       on_z(d))
 
-    def ret_a(h, d, back):
-        return remote(4, h, d, pa_send.at[h, (y + d) % N], pa.at[h, (y + N - d) % N if back else y],
+    def ret_a(h, d):
+        return remote(4, h, d, pa_send.at[h, (y + d) % N], pa.at[h, y],
                       on_y(d))
 
-    def ret_b(h, d, back):
-        return remote(5, h, d, pb_send.at[h, (z + d) % N], pb.at[h, (z + N - d) % N if back else z],
+    def ret_b(h, d):
+        return remote(5, h, d, pb_send.at[h, (z + d) % N], pb.at[h, z],
                       on_z(d))
 
-    def home_a(h, d, back):
+    def home_a(h, d):
         return remote(6, h, d, qa_send.at[h, ((z + d) % N) // NB],
-                      qa.at[(z + N - d) % N if back else z], on_z(d))
-
-    def home_b(h, d, back):
+                      qa.at[z], on_z(d))
+
+    def home_b(h, d):
         return remote(7, h, d, qb_send.at[h, ((y + d) % N) // NB],
-                      qb.at[(y + N - d) % N if back else y], on_y(d))
+                      qb.at[y], on_y(d))
 
     def hop_copy(t):
         return pltpu.make_async_remote_copy(
             src_ref=out.at[t], dst_ref=hop.at[t + 1], send_sem=hs.at[t], recv_sem=hr.at[t],
             device_id=((s + 1) % N, e), device_id_type=MESH)
 
-    def each_source(h, act):
-        first = (mine + NB - h) % NB
-        for k in range(G - 1, 0, -1):
-            act(k * NB + first)
-
-        @pl.when(first != 0)
-        def _():
-            act(first)
+    def all_of(phase, h, size):
+        return remote(phase, h, 1, size, size, on_y(1))
+
+    def many_sources(phase, h, buf):
+        @pl.when(mine == h)
+        def _():
+            all_of(phase, h, buf.at[:G - 1]).wait_recv()
+
+        @pl.when(mine != h)
+        def _():
+            all_of(phase, h, buf).wait_recv()
+
+    def many_homes(phase, h, buf):
+        @pl.when(mine == h)
+        def _():
+            all_of(phase, h, buf.at[:G - 1]).wait_send()
+
+        @pl.when(mine != h)
+        def _():
+            all_of(phase, h, buf).wait_send()
 
     def each_home(h, act):
         first = (h + NB - mine) % NB
@@ -183,8 +195,8 @@
             na[...] = n[:, :CA]
             nb[...] = n[:, CA:]
             for d in ORDER:
-                small_a(h, d, False).start()
-                small_b(h, d, False).start()
+                small_a(h, d).start()
+                small_b(h, d).start()
             sa[h, z // NB] = n[:, :CA]
             sb[h, y // NB] = n[:, CA:]
 
@@ -216,15 +228,15 @@
         lb[h] = (dot_t(gt[...], xy).reshape(N, BLK, GR) * mt[...][None]).reshape(N * BLK, GR).astype(BF)
 
     def select(h, t):
-        each_source(h, lambda d: small_a(h, d, True).wait_recv())
+        many_sources(0, h, sa.at[h])
         ba_send[h] = dot(la[h], sa[h].reshape(GR, CA)).astype(BF)
         for d in ORDER:
-            big_a(h, d, False).start()
+            big_a(h, d).start()
         ba[h, y] = ba_send[h]
-        each_source(h, lambda d: small_b(h, d, True).wait_recv())
+        many_sources(1, h, sb.at[h])
         bb_send[h] = dot(lb[h], sb[h].reshape(GR, CB)).astype(BF).reshape(N, BLK, CB)
         for d in ORDER:
-            big_b(h, d, False).start()
+            big_b(h, d).start()
         bb[h, z] = bb_send[h, z]
 
     def inward(block, first, columns):
@@ -249,8 +261,7 @@
                 load_d.wait()
                 for d in ORDER:
                     weight_copy(d, True).wait_recv()
-        for d in ORDER:
-            big_b(h, d, True).wait_recv()
+        all_of(3, h, bb.at[h, :N - 1]).wait_recv()
         proj_b = inward(bb[h], WA, CB)
         high = proj_b.astype(BF)
         low = (proj_b - high.astype(F32)).astype(BF)
@@ -258,17 +269,16 @@
         tick_lane = lax.broadcasted_iota(jnp.int32, (N * SL, 128), 1) == t
         weight = jnp.sum(jnp.where(tick_lane, wbuf[:, SL * h:SL * h + SL, :].reshape(N * SL, 128), 0.0),
                          axis=1, keepdims=True)
-        for d in ORDER:
-            big_a(h, d, True).wait_recv()
+        all_of(2, h, ba.at[h, :N - 1]).wait_recv()
         proj += inward(ba[h], 0, CA)
         gate, up = proj[:, :FF], proj[:, FF:]
         inner = (gate / (1.0 + jnp.exp(-gate)) * up * weight).astype(BF)
         pa_send[h] = outward(inner, 0, CA)
         for d in ORDER:
-            ret_a(h, d, False).start()
+            ret_a(h, d).start()
         pb_send[h] = outward(dot(perm[h], inner).astype(BF), WA, CB)
         for d in ORDER:
-            ret_b(h, d, False).start()
+            ret_b(h, d).start()
         pa[h, y] = pa_send[h, y]
         pb[h, z] = pb_send[h, z]
         xz, xy, gz = spread_hits(h, t)
@@ -277,30 +287,26 @@
 
         @pl.when(mine == h)
         def _():
-            for d in ORDER:
-                small_a(h, d, False).wait_send()
-                small_b(h, d, False).wait_send()
+            all_of(0, h, qa.at[:N - 1]).wait_send()
+            all_of(1, h, qb.at[:N - 1]).wait_send()
 
     def gather(h, t):
         @pl.when(t > 0)
         def _():
-            each_home(h, lambda d: (home_a(h, d, False).wait_send(), home_b(h, d, False).wait_send()))
-        for d in ORDER:
-            ret_b(h, d, True).wait_recv()
+            many_homes(6, h, qa_send.at[h])
+            many_homes(7, h, qb_send.at[h])
+
+        all_of(5, h, pb.at[h, :N - 1]).wait_recv()
         qb_send[h] = dot(rb[h], pb[h].reshape(N * BLK, CB)).astype(BF).reshape(G, 16, CB)
-        each_home(h, lambda d: home_b(h, d, False).start())
-        for d in ORDER:
-            ret_a(h, d, True).wait_recv()
+        each_home(h, lambda d: home_b(h, d).start())
+        all_of(4, h, pa.at[h, :N - 1]).wait_recv()
         total = pa[h, 0].astype(F32)
         for i in range(1, N):
             total += pa[h, i].astype(F32)
         qa_send[h] = dot(ra[h], total.astype(BF)).astype(BF).reshape(G, 16, CA)
-        each_home(h, lambda d: home_a(h, d, False).start())
-        for d in ORDER:
-            big_a(h, d, False).wait_send()
-            big_b(h, d, False).wait_send()
-            ret_a(h, d, False).wait_send()
-            ret_b(h, d, False).wait_send()
+        each_home(h, lambda d: home_a(h, d).start())
+        for phase, buf in ((2, ba), (3, bb), (4, pa), (5, pb)):
+            all_of(phase, h, buf.at[h, :N - 1]).wait_send()
 
     def finish(h, t):
         @pl.when(mine == h)
@@ -308,13 +314,11 @@
             qa[z] = qa_send[h, z // NB]
             qb[y] = qb_send[h, y // NB]
             x = out[t].astype(F32)
-            for d in ORDER:
-                home_b(h, d, True).wait_recv()
+            all_of(7, h, qb.at[:N - 1]).wait_recv()
             total_b = qb[0].astype(F32)
             for i in range(1, N):
                 total_b += qb[i].astype(F32)
-            for d in ORDER:
-                home_a(h, d, True).wait_recv()
+            all_of(6, h, qa.at[:N - 1]).wait_recv()
             total_a = qa[0].astype(F32)
             for i in range(1, N):
                 total_a += qa[i].astype(F32)
@@ -331,8 +335,10 @@
     hz[at(z)] = hown[...]
     hy[at(y)] = hown[...]
 
-    order = ((begin, 0, 0), (gather, 1, 1), (select, 0, 0), (finish, 1, 1), (begin, 1, 0),
-             (experts, 0, 0), (select, 1, 0), (gather, 0, 0), (experts, 1, 0), (finish, 0, 0))
+    order = ((begin, 0, 0), (begin, 1, 0), (gather, 2, 1), (gather, 3, 1), (select, 0, 0),
+             (select, 1, 0), (finish, 2, 1), (finish, 3, 1), (begin, 2, 0), (begin, 3, 0),
+             (experts, 0, 0), (experts, 1, 0), (select, 2, 0), (select, 3, 0), (gather, 0, 0),
+             (gather, 1, 0), (experts, 2, 0), (experts, 3, 0), (finish, 0, 0), (finish, 1, 0))
 
     def tick(t, carry):
         for step, h, late in order:
@@ -344,7 +350,8 @@
     lax.fori_loop(0, N + 1, tick, 0)
 
     for h in range(NB):
-        each_home(h, lambda d: (home_a(h, d, False).wait_send(), home_b(h, d, False).wait_send()))
+        many_homes(6, h, qa_send.at[h])
+        many_homes(7, h, qb_send.at[h])
     for d in ORDER:
         for c in table_copies(d, False):
             c.wait_send()
@@ -420,7 +427,7 @@
             pltpu.VMEM((NB, N, BLK, CA), BF), pltpu.VMEM((NB, N, BLK, CB), BF),
             pltpu.VMEM((NB, G, 16, CA), BF), pltpu.VMEM((NB, G, 16, CB), BF),
             pltpu.VMEM((N, 16, CA), BF), pltpu.VMEM((N, 16, CB), BF),
-            pltpu.SemaphoreType.DMA((8, NB, N)), pltpu.SemaphoreType.DMA((8, NB, N)),
+            pltpu.SemaphoreType.DMA((8, NB)), pltpu.SemaphoreType.DMA((8, NB)),
             pltpu.SemaphoreType.DMA((3, N)), pltpu.SemaphoreType.DMA((3, N)),
             pltpu.SemaphoreType.DMA((N,)), pltpu.SemaphoreType.DMA((N,)),
             pltpu.SemaphoreType.DMA((2,)),

time: 289 us -> 269 us (0.931)
  the two profiles are of different devices: /device:TPU:10 before, /device:TPU:62 now
where the time goes in v4:
time: 269 us
  Pallas kernels  264 us (98%)
  local copies, waits for them, and re-layouts  3.99 us (1%)
    pallas_call x1, Pallas kernels, body(): pl.pallas_call(kernel, out_shape=jax.ShapeDtypeStruct((N, 16, CA + CB), B...  264 us

profile of v4, /device:TPU:62, one launch (start us, length us, event | category | flops | bytes accessed | tf_op | source)
XLA Modules:
  0.0 269.0 jit_solution(17033485750949215414)
XLA Ops:
  0.0 0.7 copy.19
  0.7 0.7 copy.18
  1.4 0.1 broadcast_in_dim.12
  1.5 0.1 reshape.16
  1.5 0.6 concatenate.10.weights
  2.1 0.1 broadcast_in_dim.11
  2.2 0.1 reshape.15
  2.3 0.6 concatenate.9.picked
  2.9 264.2 %shard_map.127 = bf16[8,16,896]{2,1,0:T(8,128)(2,1)} custom-call(bf16[15,4,3584]{2,1,0:T(4,128)(2,1)} %micro.1, bf16[1,3584]{1,0:T(2,128)(2,1)} %norm_gain.1, s32[2,8,128]{2,1,0:T(8,128)} %concatenate.9.picked, f32[2,8,128]{2,1,0:T(8,128)} %concatenate.10.weights, bf16[1,1,3584,256]{3,2,1,0:T(8,128)(2,1)} %wg_hbm.1, bf16[1,1,128,3584]{3,2,1,0:T(8,128)(2,1)} %wd_hbm.1, ...), custom_call_target="tpu_custom_call" | custom-call | tf_op jit(solution)/shard_map/pallas_call | solution.py:408
  267.1 1.0 reshape.17
  268.2 0.8 maximum_bitcast_fusion
  (2 shorter events, 0.1 us)
